TPU v7x, 256 devices: a whole 4x4x8 slice. The times are simulated.
256 devices in a mesh: fsdp: 64 (over x, y_hi, z), tp: 4 (over y_lo, core).
Axes of the slice: x: 4, y: 4 (y_hi: 2, y_lo: 2; y = y_hi * 2 + y_lo), z: 8, core: 2. Of those that a mesh axis runs over, the one named last changes fastest.
Arguments:
- activations: bfloat16 [32768, 8192], P('fsdp', 'tp'), may hold values from -6 to 6
- cotangent: bfloat16 [32768, 8192], P('fsdp', 'tp'), may hold values from -0.09375 to 0.09375
- projector: bfloat16 [8192, 1024], P(None, 'tp'), may hold values from -0.0625 to 0.0625
- first_moment: float32 [8192, 1024], P('fsdp', 'tp'), may hold values from -6 to 6
- second_moment: float32 [8192, 1024], P('fsdp', 'tp'), may hold values from 0.25 to 4
Outputs:
- weight_update: float32 [8192, 8192], P('tp', 'fsdp')
- first_new: float32 [8192, 1024], P('fsdp', 'tp')
- second_new: float32 [8192, 1024], P('fsdp', 'tp')
All inputs are finite; a program needn't handle non-finite values.
Results may differ from a plain program's by a relative error of at most 0.0029.
Values may be sent and summed in bfloat16 or wider, within the bound.
A program may use at most 128 MiB of HBM per device.

v0:
```python
import jax
import jax.numpy as jnp
from jax import lax
from jax.sharding import PartitionSpec as P


def contract_first(left_side, right_side):
    return lax.dot_general(
        left_side, right_side, (((0,), (0,)), ((), ())), preferred_element_type=jnp.float32
    )


def contract_last(left_side, right_side):
    return lax.dot_general(
        left_side, right_side, (((1,), (1,)), ((), ())), preferred_element_type=jnp.float32
    )


def body(activations, cotangent, projector, first_moment, second_moment):
    features, gradients = (
        lax.all_gather(activations, "tp", axis=1, tiled=True),
        lax.all_gather(cotangent, "tp", axis=1, tiled=True),
    )
    projected = jnp.dot(features, projector, preferred_element_type=jnp.float32).astype(
        jnp.bfloat16
    )
    selected = gradients
    grad_proj = lax.psum_scatter(
        contract_first(selected, projected), "fsdp", scatter_dimension=0, tiled=True
    )
    first_new = 0.9 * first_moment + 0.1 * grad_proj
    second_new = 0.999 * second_moment + 0.001 * grad_proj * grad_proj
    direction = (first_new / (jnp.sqrt(second_new) + 1e-08)).astype(jnp.bfloat16)
    selected = projector
    weight_update = lax.psum_scatter(
        contract_last(selected, direction), "tp", scatter_dimension=0, tiled=True
    )
    return (weight_update, first_new, second_new)


def solution(mesh):
    return jax.shard_map(
        body,
        mesh=mesh,
        in_specs=(
            P("fsdp", "tp"),
            P("fsdp", "tp"),
            P(None, "tp"),
            P("fsdp", "tp"),
            P("fsdp", "tp"),
        ),
        out_specs=(P("tp", "fsdp"), P("fsdp", "tp"), P("fsdp", "tp")),
        check_vma=False,
    )
```

profile of v0, /device:TPU:1, one launch (start us, length us, event | category | flops | bytes accessed | tf_op | source)
XLA Modules:
  0.0 640.8 jit_solution(11343612445137936248)
XLA Ops:
  7.2 0.0 all-gather.3.cloned.1.call-start
  7.2 0.7 all-gather.3.cloned.1.call-update
  7.9 0.0 all-gather.5.cloned.1.call-start
  7.9 0.7 all-gather.5.cloned.1.call-update
  8.6 0.0 reduce-scatter.3.cloned.1.call-start
  8.7 89.3 %all-gather.3.cloned.1.call-done = bf16[512,8192]{1,0:T(8,128)(2,1)} async-done(((bf16[512,2048]{1,0:T(8,128)(2,1)}), bf16[512,8192]{1,0:T(8,128)(2,1)}) %all-gather.3.cloned.1.call-update) | async-done | bytes 8388624 | tf_op jit(solution)/shard_map/all_gather | solution.py:21
  98.0 86.7 %all-gather.5.cloned.1.call-done = bf16[512,8192]{1,0:T(8,128)(2,1)} async-done(((bf16[512,2048]{1,0:T(8,128)(2,1)}), bf16[512,8192]{1,0:T(8,128)(2,1)}) %all-gather.5.cloned.1.call-update) | async-done | bytes 8388624 | tf_op jit(solution)/shard_map/all_gather | solution.py:22
  184.7 19.2 %convolution_bitcast_fusion = f32[8192,256]{0,1:T(8,128)} fusion(bf16[512,8192]{1,0:T(8,128)(2,1)} %all-gather.5.cloned.1.call-done, bf16[512,8192]{1,0:T(8,128)(2,1)} %all-gather.3.cloned.1.call-done, bf16[8192,256]{1,0:T(8,128)(2,1)} %param.7), kind=kOutput, calls=%fused_computation | convolution fusion | flops 4295098368 | bytes 29360128 | tf_op jit(solution)/shard_map/dot_general | solution.py:8
  203.9 0.0 copy-start
  203.9 0.0 copy-start.1
  203.9 0.0 reduce-scatter.3.cloned.1.call-update
  203.9 0.0 reduce-scatter.5.cloned.1.call-start
  204.0 0.8 copy-done
  204.8 0.1 copy.8
  204.9 0.0 copy-done.1
  204.9 0.1 copy.9
  205.0 332.8 %reduce-scatter.3.cloned.1.call-done = f32[128,256]{0,1:T(8,128)} async-done(((f32[8192,256]{0,1:T(8,128)}), f32[128,256]{0,1:T(8,128)}) %reduce-scatter.3.cloned.1.call-update) | async-done | bytes 131088 | tf_op jit(solution)/shard_map/reduce_scatter | solution.py:28
  537.8 0.9 fusion
  538.7 5.7 convolution_bitcast_fusion.1
  544.4 0.0 reduce-scatter.5.cloned.1.call-update
  544.4 0.8 copy.12
  545.2 0.8 copy.11
  545.9 85.8 %reduce-scatter.5.cloned.1.call-done = f32[2048,128]{0,1:T(8,128)} async-done(((f32[8192,128]{0,1:T(8,128)}), f32[2048,128]{0,1:T(8,128)}) %reduce-scatter.5.cloned.1.call-update) | async-done | bytes 1048592 | tf_op jit(solution)/shard_map/reduce_scatter | solution.py:35
  631.7 2.5 copy.10
Async XLA Ops:
  7.2 90.9 %all-gather.3.cloned.1.call-start = ((), (), s32[]{:S(2)}) async-start(), calls=%async_computation.2 | async-start | bytes 10485760 | tf_op jit(solution)/shard_map/all_gather | solution.py:21
  7.9 176.8 %all-gather.5.cloned.1.call-start = ((), (), s32[]{:S(2)}) async-start(), calls=%async_computation.3 | async-start | bytes 10485760 | tf_op jit(solution)/shard_map/all_gather | solution.py:22
  8.6 529.1 %reduce-scatter.3.cloned.1.call-start = ((), (), s32[]{:S(2)}) async-start(), calls=%async_computation.4 | async-start | bytes 8519680 | tf_op jit(solution)/shard_map/reduce_scatter | solution.py:28
  203.9 0.9 copy-start
  203.9 1.0 copy-start.1
  203.9 427.8 %reduce-scatter.5.cloned.1.call-start = ((), (), s32[]{:S(2)}) async-start(), calls=%async_computation.5 | async-start | bytes 5242880 | tf_op jit(solution)/shard_map/reduce_scatter | solution.py:35
Sparse Core Ops, SparseCore 0:
  9.8 88.1 all-gather.2
  99.8 84.8 all-gather.4
  204.1 333.6 reduce-scatter.2
  544.5 87.1 reduce-scatter.4
where the time goes:
time: 641 us
  waiting for transfers between devices  596 us (93%)
  matrix products  24.8 us (4%)
  between operations  13.8 us (2%)
    reduce_scatter x1, waiting for transfers between devices, body(): lax.psum_scatter(contract_first(selected, projected), 'fsdp', scatter_dim...  333 us
    all_gather x1, waiting for transfers between devices, body(): lax.all_gather(activations, 'tp', axis=1, tiled=True)  89.3 us
    all_gather x1, waiting for transfers between devices, body(): lax.all_gather(cotangent, 'tp', axis=1, tiled=True)  86.7 us
    reduce_scatter x1, waiting for transfers between devices, body(): lax.psum_scatter(contract_last(selected, direction), 'tp', scatter_dimens...  85.8 us
    dot_general x1, matrix products, contract_first(): lax.dot_general(left_side, right_side, (((0,), (0,)), ((), ())), preferre...  19.2 us
  transfers between devices with their start and end apart: 4, of which 4 were waited for; matrix products, arithmetic and copies ran while one was open for 0% of the time, Pallas kernels for 0%

commit v1 on v0

v1 whole, which is shorter than its diff:
```python
import jax
import jax.numpy as jnp
from jax import lax
from jax.experimental import pallas as pl
from jax.experimental.pallas import tpu as pltpu
from jax.sharding import PartitionSpec as P

MESH = pl.DeviceIdType.MESH
BF, F32 = jnp.bfloat16, jnp.float32
WA, WB = 64, 64


def device(x, y_hi, z, t):
    return (x * 16 + y_hi * 8 + z, t)


def kernel(
    a_hbm, c_hbm, p_hbm, m1_hbm, m2_hbm,
    w_out, f_out, s_out,
    a_v, c_v, ct_v, p_v, m1_v, m2_v,
    hold, core_out, core_in, y_out, y_in, proj,
    ga, gb, xin, fa, zb1, zb2, za1, za2, fb, ra, rb, dirs,
    lsem, psend, precv, esend, erecv, xsend, xrecv,
    zbsend, zbrecv, zasend, zarecv, rasend, rarecv, rbsend, rbrecv, dsend, drecv,
):
    f = lax.axis_index("fsdp")
    t = lax.axis_index("tp")
    x, y_hi, z = f // 16, (f // 8) % 2, f % 8
    y_lo, c = t // 2, t % 2
    y = y_hi * 2 + y_lo

    def at_y(step, core):
        yy = lax.rem(y + step + 4, 4)
        return device(x, yy // 2, z, (yy % 2) * 2 + core)

    def at_x(step):
        return device(lax.rem(x + step + 4, 4), y_hi, z, t)

    def at_z(step):
        return device(x, y_hi, lax.rem(z + step + 8, 8), t)

    other_core = device(x, y_hi, z, y_lo * 2 + 1 - c)
    y_partner = device(x, y_hi, z, (1 - y_lo) * 2 + c)

    def remote(src, dst, ss, rs, dev):
        return pltpu.make_async_remote_copy(
            src_ref=src, dst_ref=dst, send_sem=ss, recv_sem=rs, device_id=dev, device_id_type=MESH
        )

    even = x % 2 == 0
    inner = (x == 0) | (x == 3)
    pairs = [
        (jnp.where(inner, 1, 0), jnp.where(inner, 2, 3)),
        (jnp.where(inner, 0, 1), jnp.where(inner, 3, 2)),
    ]

    loads = [
        pltpu.make_async_copy(a_hbm, a_v, lsem.at[0]),
        pltpu.make_async_copy(c_hbm, c_v, lsem.at[1]),
        pltpu.make_async_copy(p_hbm.at[pl.ds(t * 2048, 2048)], p_v.at[t], lsem.at[2]),
        pltpu.make_async_copy(m1_hbm, m1_v, lsem.at[3]),
        pltpu.make_async_copy(m2_hbm, m2_v, lsem.at[4]),
    ]
    for load in loads:
        load.start()

    barrier = pltpu.get_barrier_semaphore()
    partners = [other_core, at_x(1), at_x(-1), at_z(1), at_z(-1)]
    partners += [at_y(s, k) for s in (1, -1) for k in (0, 1)]
    for dev in partners:
        pl.semaphore_signal(barrier, inc=1, device_id=dev, device_id_type=MESH)
    for xs in range(4):
        for yh in range(2):
            @pl.when(jnp.logical_not((xs == x) & (x == t) & (yh == y_hi)))
            def _():
                pl.semaphore_signal(
                    barrier, inc=1, device_id=device(xs, yh, z, x), device_id_type=MESH
                )

    pl.semaphore_wait(barrier, len(partners) + 8 - jnp.where(x == t, 1, 0))

    p_core = remote(
        p_hbm.at[pl.ds((y_lo * 2 + 1 - c) * 2048, 2048)], p_v.at[t], psend.at[4], precv.at[4], other_core
    )
    p_core.start()

    def p_send(side, core):
        base = ((1 - y_lo) * 2 + core) * 2048 + side * 1024
        return remote(
            p_hbm.at[pl.ds(base, 1024)],
            p_v.at[t, pl.ds(side * 1024, 1024)],
            psend.at[side * 2 + core],
            precv.at[side * 2 + c],
            at_y(1 if side == 0 else -1, core),
        )

    def p_recv(side, core_from):
        slot = p_v.at[(1 - y_lo) * 2 + core_from, pl.ds(side * 1024, 1024)]
        return remote(slot, slot, psend.at[0], precv.at[side * 2 + core_from], other_core)

    def p_sends(h):
        own = (pairs[h][0] == t) | (pairs[h][1] == t)

        @pl.when(own)
        def _():
            for side in range(2):
                for core in range(2):
                    p_send(side, core).start()

    p_sends(0)

    loads[1].wait()

    @pl.loop(0, 8)
    def _(i):
        o = pl.multiple_of(i * 256, 256)
        ct_v[pl.ds(o, 256), :] = c_v[:, pl.ds(o, 256)].T

    loads[0].wait()
    loads[2].wait()

    def dot_partial(q, keep):
        @pl.loop(0, 2)
        def _(i):
            rows = pl.ds(pl.multiple_of(i * 256, 256), 256)
            acc = jnp.dot(a_v[rows, :], p_v[q], preferred_element_type=F32)
            if keep:
                hold[rows, :] = acc
            else:
                core_out[rows, :] = acc.astype(BF)

    def project(h):
        mine = pairs[h]
        q_local = jnp.where(y_lo == 0, mine[0], mine[1])
        q_far = jnp.where(y_lo == 0, mine[1], mine[0])
        to_core = remote(core_out, core_in.at[h], esend.at[h, 0], erecv.at[h, 0], other_core)
        to_y = remote(y_out.at[h], y_in.at[h], esend.at[h, 1], erecv.at[h, 1], y_partner)
        to_core2 = remote(proj.at[h, c], proj.at[h, c], esend.at[h, 2], erecv.at[h, 2], other_core)

        def keep_and_send(q):
            dot_partial(q, True)
            to_core.wait_recv()
            hold[...] = hold[...] + core_in[h].astype(F32)
            y_out[h] = hold[...].astype(BF)
            to_y.start()

        def give(q):
            dot_partial(q, False)
            to_core.start()

        first = c == y_lo
        if h == 0:
            @pl.when(q_local != t)
            def _():
                p_core.wait_recv()
        else:
            @pl.when(q_local != t)
            def _():
                p_core.wait_recv()

        @pl.when(first)
        def _():
            keep_and_send(q_local)

        @pl.when(jnp.logical_not(first))
        def _():
            give(q_local)

        far_core = q_far % 2
        for side in range(2):
            p_recv(side, far_core).wait_recv()
        if h == 0:
            p_sends(1)

        @pl.when(first)
        def _():
            give(q_far)

        @pl.when(jnp.logical_not(first))
        def _():
            keep_and_send(q_far)

        to_y.wait_recv()
        proj[h, c] = (hold[...] + y_in[h].astype(F32)).astype(BF)
        to_core2.start()
        to_core.wait_send()
        to_core2.wait_recv()
        return to_y, to_core2

    def gradient(h, slot):
        q = pairs[h][slot]

        @pl.loop(0, 8)
        def _(i):
            rows = pl.ds(pl.multiple_of(i * 256, 256), 256)
            acc = jnp.dot(ct_v[rows, :], proj[h, slot], preferred_element_type=F32)
            both = acc.astype(BF).reshape(2, 128, 256)
            for k in range(2):
                j = i * 2 + k
                ga[q, j] = both[k, :WA]
                gb[h, j % 8, j // 8, slot] = both[k, WA:]

    def half_of(d):
        return d

    def xq(d, n):
        step = jnp.where(d == 0, n, -n)
        return lax.rem(x + step + 4, 4)

    def x_to(d):
        return device(lax.rem(x + jnp.where(d == 0, 1, 3), 4), y_hi, z, t)

    def x_msg(d, m):
        if m == 0:
            q, half = xq(d, 2), d
        elif m == 1:
            q, half = xq(d, 1), 1 - d
        else:
            q, half = xq(d, 1), d
        src = ga.at[q, pl.ds(half * 8, 8)]
        return remote(src, xin.at[d, m], xsend.at[d, m], xrecv.at[d, m], x_to(d))

    def x_sum(d):
        x_msg(d, 0).wait_recv()
        q = xq(d, 1)
        for k in range(8):
            j = d * 8 + k
            ga[q, j] = (ga[q, j].astype(F32) + xin[d, 0, k].astype(F32)).astype(BF)
        x_msg(d, 2).start()

    def zc(d, n):
        return lax.rem(z + (n if d == 0 else 8 - n), 8)

    def zb_msg(h, d, m):
        if m == 0:
            return remote(
                gb.at[h, zc(d, 4), d], zb1.at[h, d], zbsend.at[h, d, 0], zbrecv.at[h, d, 0],
                at_z(1 if d == 0 else -1),
            )
        return remote(
            gb.at[h, zc(d, 4 - m)], zb2.at[h, d, m - 1], zbsend.at[h, d, m], zbrecv.at[h, d, m],
            at_z(1 if d == 0 else -1),
        )

    def zb_step(h, d, m):
        zb_msg(h, d, m - 1).wait_recv()
        if m == 1:
            tgt = gb.at[h, zc(d, 3), d]
            tgt[...] = (tgt[...].astype(F32) + zb1[h, d].astype(F32)).astype(BF)
        else:
            tgt = gb.at[h, zc(d, 4 - m)]
            tgt[...] = (tgt[...].astype(F32) + zb2[h, d, m - 2].astype(F32)).astype(BF)
        zb_msg(h, d, m).start()

    def za_msg(d, m):
        if m == 0:
            return remote(
                fa.at[zc(d, 4), d], za1.at[d], zasend.at[d, 0], zarecv.at[d, 0],
                at_z(1 if d == 0 else -1),
            )
        return remote(
            fa.at[zc(d, 4 - m)], za2.at[d, m - 1], zasend.at[d, m], zarecv.at[d, m],
            at_z(1 if d == 0 else -1),
        )

    def za_step(d, m):
        za_msg(d, m - 1).wait_recv()
        if m == 1:
            tgt = fa.at[zc(d, 3), d]
            tgt[...] = (tgt[...].astype(F32) + za1[d].astype(F32)).astype(BF)
        else:
            tgt = fa.at[zc(d, 4 - m)]
            tgt[...] = (tgt[...].astype(F32) + za2[d, m - 2].astype(F32)).astype(BF)
        za_msg(d, m).start()

    def mine_a(yh):
        return (x == t) & (yh == y_hi)

    def mine_b(yh, q):
        return (x == t) & (yh == y_hi) & (q == t)

    def ra_msg(yh):
        return remote(fa.at[z, yh], ra.at[y_hi], rasend.at[yh], rarecv.at[y_hi], device(t, yh, z, x))

    def rb_msg(h, slot, yh):
        q = pairs[h][slot]
        return remote(
            fb.at[h, yh, slot], rb.at[x * 2 + y_hi], rbsend.at[h, slot, yh], rbrecv.at[x * 2 + y_hi],
            device(t, yh, z, q),
        )

    def zb_final(h):
        for d in range(2):
            zb_msg(h, d, 3).wait_recv()
        fb[h] = (
            gb[h, z].astype(F32) + zb2[h, 0, 2].astype(F32) + zb2[h, 1, 2].astype(F32)
        ).astype(BF)
        for slot in range(2):
            q = pairs[h][slot]
            for yh in range(2):
                own = mine_b(yh, q)

                @pl.when(own)
                def _():
                    rb[x * 2 + y_hi] = fb[h, yh, slot]

                @pl.when(jnp.logical_not(own))
                def _():
                    rb_msg(h, slot, yh).start()

    exch0 = project(0)
    first_slot = lax.rem(x + 2, 4)
    for slot in range(2):
        gradient(0, slot)
    near = jnp.where(even, 0, 1)
    far = 1 - near
    for d in range(2):
        x_msg(d, 0).start()
        zb_msg(0, d, 0).start()
    x_msg(near, 1).start()
    exch1 = project(1)
    x_sum(near)
    for d in range(2):
        zb_step(0, d, 1)
    for slot in range(2):
        gradient(1, slot)
    x_msg(far, 1).start()
    x_sum(far)
    for d in range(2):
        zb_msg(1, d, 0).start()
    for m in (2, 3):
        for d in range(2):
            zb_step(0, d, m)
        for d in range(2):
            zb_step(1, d, m - 1)
    for d in range(2):
        zb_step(1, d, 3)
    zb_final(0)

    for d in range(2):
        x_msg(d, 1).wait_recv()
        x_msg(d, 2).wait_recv()
    for yh in range(2):
        for k in range(8):
            fa[k, yh] = (
                ga[x, yh * 8 + k].astype(F32)
                + xin[yh, 2, k].astype(F32)
                + xin[1 - yh, 1, k].astype(F32)
            ).astype(BF)
    for d in range(2):
        za_msg(d, 0).start()
    zb_final(1)
    for m in (1, 2, 3):
        for d in range(2):
            za_step(d, m)
    for d in range(2):
        za_msg(d, 3).wait_recv()
    fa[z] = (fa[z].astype(F32) + za2[0, 2].astype(F32) + za2[1, 2].astype(F32)).astype(BF)
    for yh in range(2):
        own = mine_a(yh)

        @pl.when(own)
        def _():
            ra[y_hi] = fa[z, yh]

        @pl.when(jnp.logical_not(own))
        def _():
            ra_msg(yh).start()

    def ra_wait(s):
        remote(ra.at[s], ra.at[s], rasend.at[0], rarecv.at[s], other_core).wait_recv()

    def rb_wait(s):
        remote(rb.at[s], rb.at[s], rbsend.at[0, 0, 0], rbrecv.at[s], other_core).wait_recv()

    for xs in range(4):
        for yh in range(2):
            @pl.when(jnp.logical_not((xs == x) & (x == t) & (yh == y_hi)))
            def _():
                rb_wait(xs * 2 + yh)
    for yh in range(2):
        @pl.when(jnp.logical_not(mine_a(yh)))
        def _():
            ra_wait(yh)

    loads[3].wait()
    loads[4].wait()
    up = ra[0].astype(F32) + ra[1].astype(F32)
    down = rb[0].astype(F32)
    for s in range(1, 8):
        down = down + rb[s].astype(F32)
    for rows, g in ((pl.ds(0, WA), up), (pl.ds(WA, WB), down)):
        first_new = 0.9 * m1_v[rows, :] + 0.1 * g
        second_new = 0.999 * m2_v[rows, :] + 0.001 * g * g
        f_out[rows, :] = first_new
        s_out[rows, :] = second_new
        dirs[t, rows, :] = (first_new / (jnp.sqrt(second_new) + 1e-08)).astype(BF)

    def d_msg(k):
        return remote(
            dirs.at[t], dirs.at[t], dsend.at[k], drecv.at[k], (f, lax.rem(t + k, 4))
        )

    def d_wait(k):
        slot = dirs.at[lax.rem(t + 4 - k, 4)]
        remote(slot, slot, dsend.at[k], drecv.at[k], other_core).wait_recv()

    for k in (1, 2, 3):
        d_msg(k).start()
    for k in (1, 2, 3):
        d_wait(k)

    @pl.loop(0, 8)
    def _(i):
        rows = pl.ds(pl.multiple_of(i * 256, 256), 256)
        acc = jnp.zeros((256, 128), F32)
        for q in range(4):
            acc = acc + lax.dot_general(
                p_v[q, rows, :], dirs[q], (((1,), (1,)), ((), ())), preferred_element_type=F32
            )
        w_out[rows, :] = acc

    p_core.wait_send()
    for side in range(2):
        for core in range(2):
            p_send(side, core).wait_send()
    for to_y, to_core2 in (exch0, exch1):
        to_y.wait_send()
        to_core2.wait_send()
    for d in range(2):
        for m in range(3):
            x_msg(d, m).wait_send()
        for m in range(4):
            zb_msg(0, d, m).wait_send()
            zb_msg(1, d, m).wait_send()
            za_msg(d, m).wait_send()
    for yh in range(2):
        @pl.when(jnp.logical_not(mine_a(yh)))
        def _():
            ra_msg(yh).wait_send()

        for h in range(2):
            for slot in range(2):
                @pl.when(jnp.logical_not(mine_b(yh, pairs[h][slot])))
                def _():
                    rb_msg(h, slot, yh).wait_send()
    for k in (1, 2, 3):
        d_msg(k).wait_send()


def body(activations, cotangent, projector, first_moment, second_moment):
    dma = pltpu.SemaphoreType.DMA
    vm = pltpu.VMEM
    return pl.pallas_call(
        kernel,
        name="galore_step",
        out_shape=(
            jax.ShapeDtypeStruct((2048, 128), F32),
            jax.ShapeDtypeStruct((128, 256), F32),
            jax.ShapeDtypeStruct((128, 256), F32),
        ),
        in_specs=[pl.BlockSpec(memory_space=pl.ANY)] * 5,
        out_specs=(pl.BlockSpec(memory_space=pltpu.VMEM),) * 3,
        scratch_shapes=[
            vm((512, 2048), BF),
            vm((512, 2048), BF),
            vm((2048, 512), BF),
            vm((4, 2048, 256), BF),
            vm((128, 256), F32),
            vm((128, 256), F32),
            vm((512, 256), F32),
            vm((512, 256), BF),
            vm((2, 512, 256), BF),
            vm((2, 512, 256), BF),
            vm((2, 512, 256), BF),
            vm((2, 2, 512, 256), BF),
            vm((4, 16, WA, 256), BF),
            vm((2, 8, 2, 2, WB, 256), BF),
            vm((2, 3, 8, WA, 256), BF),
            vm((8, 2, WA, 256), BF),
            vm((2, 2, 2, WB, 256), BF),
            vm((2, 2, 3, 2, 2, WB, 256), BF),
            vm((2, WA, 256), BF),
            vm((2, 3, 2, WA, 256), BF),
            vm((2, 2, 2, WB, 256), BF),
            vm((2, WA, 256), BF),
            vm((8, WB, 256), BF),
            vm((4, 128, 256), BF),
            dma((5,)),
            dma((5,)), dma((5,)),
            dma((2, 3)), dma((2, 3)),
            dma((2, 3)), dma((2, 3)),
            dma((2, 2, 4)), dma((2, 2, 4)),
            dma((2, 4)), dma((2, 4)),
            dma((2,)), dma((2,)),
            dma((2, 2, 2)), dma((8,)),
            dma((4,)), dma((4,)),
        ],
        compiler_params=pltpu.CompilerParams(
            collective_id=0, has_side_effects=True, vmem_limit_bytes=48 << 20
        ),
        cost_estimate=pl.CostEstimate(
            flops=4_800_000_000, bytes_accessed=10 << 20, transcendentals=32768
        ),
    )(activations, cotangent, projector, first_moment, second_moment)


def solution(mesh):
    return jax.shard_map(
        body,
        mesh=mesh,
        in_specs=(
            P("fsdp", "tp"),
            P("fsdp", "tp"),
            P(None, "tp"),
            P("fsdp", "tp"),
            P("fsdp", "tp"),
        ),
        out_specs=(P("tp", "fsdp"), P("fsdp", "tp"), P("fsdp", "tp")),
        check_vma=False,
    )
```

time: 641 us -> 114 us (0.18)
  waiting for transfers between devices: 596 us -> 0 us
  Pallas kernels: 0 us -> 106 us
  matrix products: 24.8 us -> 0 us
  between operations: 13.8 us -> 0.65 us
    reduce_scatter x2 -> x0, waiting for transfers between devices: 419 us -> none  [the longest x1 333 us: body(): lax.psum_scatter(contract_first(selected, projected), 'fsdp', scatter_dim...]
    all_gather x2 -> x0, waiting for transfers between devices: 176 us -> none  [the longest x1 89.3 us: body(): lax.all_gather(activations, 'tp', axis=1, tiled=True)]
    pallas_call x0 -> x1, Pallas kernels: none -> 106 us  [body(): pl.pallas_call(kernel, name='galore_step', out_shape=(jax.ShapeDtypeStruc...]
    dot_general x2 -> x0, matrix products: 24.8 us -> none  [the longest x1 19.2 us: contract_first(): lax.dot_general(left_side, right_side, (((0,), (0,)), ((), ())), preferre...]
  transfers between devices with their start and end apart: 4 -> 0, of which waited for: 4 -> 0; matrix products, arithmetic and copies ran while one was open for 0% -> 0% of each run, Pallas kernels for 0% -> 0%
where the time goes in v1:
time: 114 us
  Pallas kernels  106 us (93%)
  local copies, waits for them, and re-layouts  7.26 us (6%)
    pallas_call x1, Pallas kernels, body(): pl.pallas_call(kernel, name='galore_step', out_shape=(jax.ShapeDtypeStruc...  106 us
    unnamed x11, local copies, waits for them, and re-layouts  7.26 us

profile of v1, /device:TPU:1, one launch (start us, length us, event | category | flops | bytes accessed | tf_op | source)
XLA Modules:
  0.0 113.6 jit_solution(8841415965602752800)
XLA Ops:
  0.6 0.0 copy-start
  0.6 1.6 %copy-done = bf16[512,2048]{1,0:T(8,128)(2,1)S(1)} copy-done((bf16[512,2048]{1,0:T(8,128)(2,1)S(1)}, bf16[512,2048]{1,0:T(8,128)(2,1)}, u32[]{:S(2)}) %copy-start) | copy-done | bytes 2097176
  2.2 0.0 copy-start.1
  2.2 1.6 %copy-done.1 = bf16[512,2048]{1,0:T(8,128)(2,1)S(1)} copy-done((bf16[512,2048]{1,0:T(8,128)(2,1)S(1)}, bf16[512,2048]{1,0:T(8,128)(2,1)}, u32[]{:S(2)}) %copy-start.1) | copy-done | bytes 2097176
  3.8 0.0 copy-start.2
  3.8 0.9 copy-done.2
  4.7 0.0 copy-start.3
  4.7 0.9 copy-done.3
  5.6 105.7 %galore_step.1 = (f32[2048,128]{1,0:T(8,128)S(1)}, f32[128,256]{1,0:T(8,128)S(1)}, f32[128,256]{1,0:T(8,128)S(1)}) custom-call(bf16[512,2048]{1,0:T(8,128)(2,1)S(1)} %copy-done, bf16[512,2048]{1,0:T(8,128)(2,1)S(1)} %copy-done.1, bf16[8192,256]{1,0:T(8,128)(2,1)} %p_hbm.1, f32[128,256]{1,0:T(8,128)S(1)} %copy-done.2, f32[128,256]{1,0:T(8,128)S(1)} %copy-done.3), custom_call_target="tpu_custom_call" | custom-call | flops 4800000000 | bytes 10485760 | tf_op jit(solution)/shard_map/galore_step/pallas_call | solution.py:454
  111.3 1.0 copy.11
  112.3 0.7 copy.12
  113.0 0.7 copy.13
Async XLA Ops:
  0.6 1.6 %copy-start = (bf16[512,2048]{1,0:T(8,128)(2,1)S(1)}, bf16[512,2048]{1,0:T(8,128)(2,1)}, u32[]{:S(2)}) copy-start(bf16[512,2048]{1,0:T(8,128)(2,1)} %a_hbm.1) | copy-start | bytes 6291460
  2.2 1.6 %copy-start.1 = (bf16[512,2048]{1,0:T(8,128)(2,1)S(1)}, bf16[512,2048]{1,0:T(8,128)(2,1)}, u32[]{:S(2)}) copy-start(bf16[512,2048]{1,0:T(8,128)(2,1)} %c_hbm.1) | copy-start | bytes 6291460
  3.8 0.9 copy-start.2
  4.7 0.9 copy-start.3

commit v2 on v0

v2 whole, which is shorter than its diff:
```python
import jax
import jax.numpy as jnp
from jax import lax
from jax.experimental import pallas as pl
from jax.experimental.pallas import tpu as pltpu
from jax.sharding import PartitionSpec as P

MESH = pl.DeviceIdType.MESH
BF, F32 = jnp.bfloat16, jnp.float32
WA = 64
WB = 128 - WA
SHARED = 352
DIRECT = 2048 - 4 * SHARED
NEAR = 256


def device(x, y_hi, z, t):
    return (x * 16 + y_hi * 8 + z, t)


def kernel(
    a_hbm, c_hbm, p_hbm, m1_hbm, m2_hbm,
    w_out, f_out, s_out,
    a_v, c_v, ct_v, p_own, p_v, m1_v, m2_v,
    hold, core_out, core_in, y_out, y_in, proj,
    ga, gb, xin, fa, zb1, zb2, za1, za2, fb, ra, rb, dirs,
    lsem, pcsend, pcrecv, pysend, pyrecv, prsend, prrecv, esend, erecv, xsend, xrecv,
    zbsend, zbrecv, zasend, zarecv, rasend, rarecv, rbsend, rbrecv, dsend, drecv,
):
    f = lax.axis_index("fsdp")
    t = lax.axis_index("tp")
    x, y_hi, z = f // 16, (f // 8) % 2, f % 8
    y_lo, c = t // 2, t % 2
    near_y = y_hi * 2 + 1 - y_lo
    other_y = lax.rem(y_hi * 2 + y_lo + jnp.where(y_lo == 0, 3, 1), 4)

    def at_side(side, core):
        yy = near_y if side == 0 else other_y
        return device(x, yy // 2, z, (yy % 2) * 2 + core)

    def at_x(d):
        return device(lax.rem(x + (1 if d == 0 else 3), 4), y_hi, z, t)

    def at_z(d):
        return device(x, y_hi, lax.rem(z + (1 if d == 0 else 7), 8), t)

    other_core = device(x, y_hi, z, y_lo * 2 + 1 - c)
    y_partner = device(x, y_hi, z, (1 - y_lo) * 2 + c)

    def remote(src, dst, ss, rs, dev):
        return pltpu.make_async_remote_copy(
            src_ref=src, dst_ref=dst, send_sem=ss, recv_sem=rs, device_id=dev, device_id_type=MESH
        )

    own_rows = pl.ds(pl.multiple_of(t * 2048, 2048), 2048)
    loads = [
        pltpu.make_async_copy(p_hbm, p_own, lsem.at[0]),
        pltpu.make_async_copy(a_hbm, a_v, lsem.at[1]),
        pltpu.make_async_copy(c_hbm, c_v, lsem.at[2]),
        pltpu.make_async_copy(p_hbm.at[own_rows, pl.ds(0, 128)], p_v.at[0, t], lsem.at[3]),
        pltpu.make_async_copy(p_hbm.at[own_rows, pl.ds(128, 128)], p_v.at[1, t], lsem.at[4]),
        pltpu.make_async_copy(m1_hbm, m1_v, lsem.at[5]),
        pltpu.make_async_copy(m2_hbm, m2_v, lsem.at[6]),
    ]
    for load in loads:
        load.start()

    barrier = pltpu.get_barrier_semaphore()
    partners = [other_core, at_x(0), at_x(1), at_z(0), at_z(1)]
    partners += [at_side(s, k) for s in range(2) for k in range(2)]
    for dev in partners:
        pl.semaphore_signal(barrier, inc=1, device_id=dev, device_id_type=MESH)
    for xs in range(4):
        for yh in range(2):
            @pl.when(jnp.logical_not((xs == x) & (x == t) & (yh == y_hi)))
            def _():
                pl.semaphore_signal(
                    barrier, inc=1, device_id=device(xs, yh, z, x), device_id_type=MESH
                )

    pl.semaphore_wait(barrier, len(partners) + 8 - jnp.where(x == t, 1, 0))

    def p_core(h):
        rows = pl.ds(pl.multiple_of((y_lo * 2 + 1 - c) * 2048, 2048), 2048)
        return remote(
            p_own.at[rows, pl.ds(h * 128, 128)], p_v.at[h, t], pcsend.at[h], pcrecv.at[h], other_core
        )

    def rows_of(kind, side, other):
        if kind == 2:
            return pl.ds(4 * SHARED + side * NEAR, NEAR if side == 0 else DIRECT - NEAR)
        parity = z % 2 if kind == 0 else x % 2
        if other:
            parity = 1 - parity
        base = kind * 2 * SHARED + parity * SHARED + side * (SHARED // 2)
        return pl.ds(pl.multiple_of(base, 16), SHARED // 2)

    def p_y(h, kind, side, core):
        rows = rows_of(kind, side, False)
        target = (1 - y_lo) * 2 + core
        src = pl.ds(pl.multiple_of(target * 2048 + rows.start, 16), rows.size)
        return remote(
            p_own.at[src, pl.ds(h * 128, 128)], p_v.at[h, t, rows],
            pysend.at[h, kind, side, core], pyrecv.at[h, kind, side, c], at_side(side, core),
        )

    def p_y_wait(h, kind, side, core):
        slot = p_v.at[h, (1 - y_lo) * 2 + core, rows_of(kind, side, False)]
        remote(slot, slot, pysend.at[h, kind, side, core], pyrecv.at[h, kind, side, core], other_core).wait_recv()

    def p_relay(h, kind, side, core):
        slot = p_v.at[h, (1 - y_lo) * 2 + core, rows_of(kind, side, False)]
        return remote(
            slot, slot, prsend.at[h, kind, side, core], prrecv.at[h, kind, side, core],
            at_z(side) if kind == 0 else at_x(side),
        )

    def p_relay_wait(h, kind, side, core):
        slot = p_v.at[h, (1 - y_lo) * 2 + core, rows_of(kind, side, True)]
        remote(slot, slot, prsend.at[h, kind, side, core], prrecv.at[h, kind, side, core], other_core).wait_recv()

    each = [(core, kind, side) for core in range(2) for kind in range(2) for side in range(2)]

    whole = [(core, 2, side) for core in range(2) for side in range(2)]

    def p_first(h):
        for core, kind, side in each:
            p_y(h, kind, side, core).start()

    def p_second(h):
        for core, kind, side in each:
            p_y(h, kind, side, core).wait_send()
        for core, kind, side in whole:
            p_y(h, kind, side, core).start()

    def p_relays(h):
        for core, kind, side in each:
            p_y_wait(h, kind, side, core)
            p_relay(h, kind, side, core).start()

    def p_arrive(h):
        for core, kind, side in whole:
            p_y_wait(h, kind, side, core)
        for core, kind, side in each:
            p_relay_wait(h, kind, side, core)

    def slot_of(e):
        return y_lo if e == 0 else 1 - y_lo

    def to_core(h, e):
        return remote(core_out.at[h, e], core_in.at[h, e], esend.at[0, h, e], erecv.at[0, h, e], other_core)

    def to_y(h, e):
        return remote(
            y_out.at[h, e], y_in.at[h, 1 - e], esend.at[1, h, e], erecv.at[1, h, 1 - e], y_partner
        )

    def y_wait(h, e):
        remote(y_out.at[h, e], y_in.at[h, e], esend.at[1, h, e], erecv.at[1, h, e], y_partner).wait_recv()

    def share(h, e):
        block = proj.at[h, slot_of(e) * 2 + c]
        return remote(block, block, esend.at[2, h, e], erecv.at[2, h, e], other_core)

    def share_wait(h, e):
        block = proj.at[h, slot_of(e) * 2 + 1 - c]
        remote(block, block, esend.at[2, h, e], erecv.at[2, h, e], other_core).wait_recv()

    def partial(h, e):
        s = slot_of(e)
        weights = jnp.concatenate([p_v[h, s * 2], p_v[h, s * 2 + 1]], axis=1)
        acc = jnp.dot(a_v[...], weights, preferred_element_type=F32)
        low, high = acc[:, :128], acc[:, 128:]
        hold[h, e] = jnp.where(c == 0, low, high)
        core_out[h, e] = jnp.where(c == 0, high, low).astype(BF)
        to_core(h, e).start()

    def chip_sum(h, e):
        to_core(h, e).wait_recv()
        total = hold[h, e] + core_in[h, e].astype(F32)
        hold[h, e] = total
        y_out[h, e] = total.astype(BF)

    def finish(h, e):
        y_wait(h, e)
        proj[h, slot_of(e) * 2 + c] = (hold[h, e] + y_in[h, e].astype(F32)).astype(BF)
        share(h, e).start()

    def gradient(h, e):
        share_wait(h, e)
        s = slot_of(e)

        @pl.loop(0, 4)
        def _(i):
            rows = pl.ds(pl.multiple_of(i * 512, 512), 512)
            right = jnp.concatenate([proj[h, s * 2], proj[h, s * 2 + 1]], axis=1)
            acc = jnp.dot(ct_v[rows, :], right, preferred_element_type=F32).astype(BF)
            blocks = acc.reshape(4, 128, 256)
            for k in range(4):
                for q in range(2):
                    part = blocks[k, :, q * 128:(q + 1) * 128]
                    ga[h, s * 2 + q, i * 4 + k] = part[:WA]
                    gb[h, (i % 2) * 4 + k, i // 2, s * 2 + q] = part[WA:]

    def add(ref, *others):
        total = ref[...].astype(F32)
        for other in others:
            total = total + other[...].astype(F32)
        ref[...] = total.astype(BF)

    def xq(d, n):
        return lax.rem(x + (n if d == 0 else 4 - n), 4)

    def x_msg(h, d, m):
        q, half = (xq(d, 2), d) if m == 0 else (xq(d, 1), 1 - d) if m == 1 else (xq(d, 1), d)
        src = ga.at[h, q, pl.ds(half * 8, 8)]
        return remote(src, xin.at[h, d, m], xsend.at[h, d, m], xrecv.at[h, d, m], at_x(d))

    def x_start(h):
        for d in range(2):
            x_msg(h, d, 0).start()

    def x_next(h):
        for d in range(2):
            x_msg(h, d, 0).wait_send()
            x_msg(h, d, 1).start()

    def x_sum(h):
        for d in range(2):
            x_msg(h, d, 0).wait_recv()
            add(ga.at[h, xq(d, 1), pl.ds(d * 8, 8)], xin.at[h, d, 0])
            x_msg(h, d, 2).start()

    def x_end(h):
        for d in range(2):
            x_msg(h, d, 1).wait_recv()
        for d in range(2):
            x_msg(h, d, 2).wait_recv()
        for yh in range(2):
            for k in range(8):
                fa[h, k, yh] = (
                    ga[h, x, yh * 8 + k].astype(F32)
                    + xin[h, yh, 2, k].astype(F32)
                    + xin[h, 1 - yh, 1, k].astype(F32)
                ).astype(BF)
        for d in range(2):
            z_msg(za, h, d, 0).start()

    def zc(d, n):
        return lax.rem(z + (n if d == 0 else 8 - n), 8)

    zb = (gb, zb1, zb2, zbsend, zbrecv)
    za = (fa, za1, za2, zasend, zarecv)

    def z_msg(ring, h, d, m):
        data, first, later, ss, rs = ring
        if m == 0:
            src, dst = data.at[h, zc(d, 4), d], first.at[h, d]
        else:
            src, dst = data.at[h, zc(d, 4 - m)], later.at[h, d, m - 1]
        return remote(src, dst, ss.at[h, d, m], rs.at[h, d, m], at_z(d))

    def z_start(ring, h):
        for d in range(2):
            z_msg(ring, h, d, 0).start()

    def z_step(ring, h, m):
        data, first, later, _, _ = ring
        for d in range(2):
            z_msg(ring, h, d, m - 1).wait_recv()
            if m == 1:
                add(data.at[h, zc(d, 3), d], first.at[h, d])
            else:
                add(data.at[h, zc(d, 4 - m)], later.at[h, d, m - 2])
            z_msg(ring, h, d, m).start()

    def mine(yh, q):
        return (x == t) & (yh == y_hi) & (q == t)

    def ra_msg(h, yh):
        return remote(
            fa.at[h, z, yh], ra.at[h, y_hi], rasend.at[h, yh], rarecv.at[h, y_hi], device(t, yh, z, x)
        )

    def rb_msg(h, q, yh):
        s = x * 2 + y_hi
        return remote(
            fb.at[h, yh, q], rb.at[h, s], rbsend.at[h, q, yh], rbrecv.at[h, s], device(t, yh, z, q)
        )

    def zb_end(h):
        for d in range(2):
            z_msg(zb, h, d, 3).wait_recv()
        fb[h] = (
            gb[h, z].astype(F32) + zb2[h, 0, 2].astype(F32) + zb2[h, 1, 2].astype(F32)
        ).astype(BF)
        for q in range(4):
            for yh in range(2):
                own = mine(yh, q)

                @pl.when(own)
                def _():
                    rb[h, x * 2 + y_hi] = fb[h, yh, q]

                @pl.when(jnp.logical_not(own))
                def _():
                    rb_msg(h, q, yh).start()

    def za_end(h):
        for d in range(2):
            z_msg(za, h, d, 3).wait_recv()
        add(fa.at[h, z], za2.at[h, 0, 2], za2.at[h, 1, 2])
        for yh in range(2):
            own = mine(yh, x)

            @pl.when(own)
            def _():
                ra[h, y_hi] = fa[h, z, yh]

            @pl.when(jnp.logical_not(own))
            def _():
                ra_msg(h, yh).start()

    def d_msg(h, k):
        return remote(
            dirs.at[h, t], dirs.at[h, t], dsend.at[h, k], drecv.at[h, k], (f, lax.rem(t + k, 4))
        )

    def adam(h):
        for xs in range(4):
            for yh in range(2):
                s = xs * 2 + yh

                @pl.when(jnp.logical_not((xs == x) & (x == t) & (yh == y_hi)))
                def _():
                    remote(rb.at[h, s], rb.at[h, s], rbsend.at[h, 0, 0], rbrecv.at[h, s], other_core).wait_recv()
        for yh in range(2):
            @pl.when(jnp.logical_not(mine(yh, x)))
            def _():
                remote(ra.at[h, yh], ra.at[h, yh], rasend.at[h, 0], rarecv.at[h, yh], other_core).wait_recv()
        up = ra[h, 0].astype(F32) + ra[h, 1].astype(F32)
        down = rb[h, 0].astype(F32)
        for s in range(1, 8):
            down = down + rb[h, s].astype(F32)
        cols = pl.ds(h * 128, 128)
        for rows, g in ((pl.ds(0, WA), up), (pl.ds(WA, WB), down)):
            first_new = 0.9 * m1_v[rows, cols] + 0.1 * g
            second_new = 0.999 * m2_v[rows, cols] + 0.001 * g * g
            f_out[rows, cols] = first_new
            s_out[rows, cols] = second_new
            dirs[h, t, rows, :] = (first_new / (jnp.sqrt(second_new) + 1e-08)).astype(BF)
        for k in (1, 2, 3):
            d_msg(h, k).start()

    def update(h):
        for k in (1, 2, 3):
            slot = dirs.at[h, lax.rem(t + 4 - k, 4)]
            remote(slot, slot, dsend.at[h, k], drecv.at[h, k], other_core).wait_recv()

        @pl.loop(0, 4)
        def _(i):
            rows = pl.ds(pl.multiple_of(i * 512, 512), 512)
            left = jnp.concatenate([p_v[h, q, rows, :] for q in range(4)], axis=1)
            right = jnp.concatenate([dirs[h, q] for q in range(4)], axis=1)
            acc = lax.dot_general(left, right, (((1,), (1,)), ((), ())), preferred_element_type=F32)
            if h == 0:
                w_out[rows, :] = acc
            else:
                w_out[rows, :] = w_out[rows, :] + acc

    loads[0].wait()
    p_first(0)
    p_core(0).start()
    p_core(1).start()
    loads[2].wait()

    @pl.loop(0, 4)
    def _(i):
        o = pl.multiple_of(i * 512, 512)
        ct_v[pl.ds(o, 512), :] = c_v[:, pl.ds(o, 512)].T

    p_second(0)
    loads[1].wait()
    loads[3].wait()
    p_core(0).wait_recv()
    partial(0, 0)
    p_relays(0)
    chip_sum(0, 0)
    to_y(0, 0).start()
    loads[4].wait()
    p_core(1).wait_recv()
    partial(1, 0)
    chip_sum(1, 0)
    p_arrive(0)
    p_first(1)
    partial(0, 1)
    chip_sum(0, 1)
    to_y(0, 1).start()
    finish(0, 1)
    p_second(1)
    gradient(0, 1)
    p_relays(1)
    finish(0, 0)
    to_y(1, 0).start()
    gradient(0, 0)
    x_start(0)
    z_start(zb, 0)
    p_arrive(1)
    partial(1, 1)
    chip_sum(1, 1)
    to_y(1, 1).start()
    finish(1, 1)
    x_next(0)
    z_step(zb, 0, 1)
    gradient(1, 1)
    x_sum(0)
    finish(1, 0)
    z_step(zb, 0, 2)
    gradient(1, 0)
    x_start(1)
    z_start(zb, 1)
    x_end(0)
    z_step(zb, 0, 3)
    x_next(1)
    z_step(zb, 1, 1)
    x_sum(1)
    z_step(za, 0, 1)
    zb_end(0)
    z_step(zb, 1, 2)
    z_step(za, 0, 2)
    x_end(1)
    z_step(zb, 1, 3)
    z_step(za, 0, 3)
    z_step(za, 1, 1)
    za_end(0)
    z_step(za, 1, 2)
    zb_end(1)
    z_step(za, 1, 3)
    loads[5].wait()
    loads[6].wait()
    adam(0)
    za_end(1)
    update(0)
    adam(1)
    update(1)

    for h in range(2):
        p_core(h).wait_send()
        for core, kind, side in whole:
            p_y(h, kind, side, core).wait_send()
        for core, kind, side in each:
            p_relay(h, kind, side, core).wait_send()
        for e in range(2):
            to_core(h, e).wait_send()
            to_y(h, e).wait_send()
            share(h, e).wait_send()
        for d in range(2):
            for m in (1, 2):
                x_msg(h, d, m).wait_send()
            for m in range(4):
                z_msg(zb, h, d, m).wait_send()
                z_msg(za, h, d, m).wait_send()
        for yh in range(2):
            @pl.when(jnp.logical_not(mine(yh, x)))
            def _():
                ra_msg(h, yh).wait_send()

            for q in range(4):
                @pl.when(jnp.logical_not(mine(yh, q)))
                def _():
                    rb_msg(h, q, yh).wait_send()
        for k in (1, 2, 3):
            d_msg(h, k).wait_send()


def body(activations, cotangent, projector, first_moment, second_moment):
    dma = pltpu.SemaphoreType.DMA
    vm = pltpu.VMEM
    return pl.pallas_call(
        kernel,
        name="galore_step",
        out_shape=(
            jax.ShapeDtypeStruct((2048, 128), F32),
            jax.ShapeDtypeStruct((128, 256), F32),
            jax.ShapeDtypeStruct((128, 256), F32),
        ),
        in_specs=[pl.BlockSpec(memory_space=pltpu.HBM)] * 5,
        out_specs=(pl.BlockSpec(memory_space=pltpu.VMEM),) * 3,
        scratch_shapes=[
            vm((512, 2048), BF),
            vm((512, 2048), BF),
            vm((2048, 512), BF),
            vm((8192, 256), BF),
            vm((2, 4, 2048, 128), BF),
            vm((128, 256), F32),
            vm((128, 256), F32),
            vm((2, 2, 512, 128), F32),
            vm((2, 2, 512, 128), BF),
            vm((2, 2, 512, 128), BF),
            vm((2, 2, 512, 128), BF),
            vm((2, 2, 512, 128), BF),
            vm((2, 4, 512, 128), BF),
            vm((2, 4, 16, WA, 128), BF),
            vm((2, 8, 2, 4, WB, 128), BF),
            vm((2, 2, 3, 8, WA, 128), BF),
            vm((2, 8, 2, WA, 128), BF),
            vm((2, 2, 4, WB, 128), BF),
            vm((2, 2, 3, 2, 4, WB, 128), BF),
            vm((2, 2, WA, 128), BF),
            vm((2, 2, 3, 2, WA, 128), BF),
            vm((2, 2, 4, WB, 128), BF),
            vm((2, 2, WA, 128), BF),
            vm((2, 8, WB, 128), BF),
            vm((2, 4, 128, 128), BF),
            dma((7,)),
            dma((2,)), dma((2,)),
            dma((2, 3, 2, 2)), dma((2, 3, 2, 2)),
            dma((2, 2, 2, 2)), dma((2, 2, 2, 2)),
            dma((3, 2, 2)), dma((3, 2, 2)),
            dma((2, 2, 3)), dma((2, 2, 3)),
            dma((2, 2, 4)), dma((2, 2, 4)),
            dma((2, 2, 4)), dma((2, 2, 4)),
            dma((2, 2)), dma((2, 2)),
            dma((2, 4, 2)), dma((2, 8)),
            dma((2, 4)), dma((2, 4)),
        ],
        compiler_params=pltpu.CompilerParams(
            collective_id=0, has_side_effects=True, vmem_limit_bytes=60 << 20
        ),
        cost_estimate=pl.CostEstimate(
            flops=4_800_000_000, bytes_accessed=10 << 20, transcendentals=32768
        ),
    )(activations, cotangent, projector, first_moment, second_moment)


def solution(mesh):
    return jax.shard_map(
        body,
        mesh=mesh,
        in_specs=(
            P("fsdp", "tp"),
            P("fsdp", "tp"),
            P(None, "tp"),
            P("fsdp", "tp"),
            P("fsdp", "tp"),
        ),
        out_specs=(P("tp", "fsdp"), P("fsdp", "tp"), P("fsdp", "tp")),
        check_vma=False,
    )
```

time: 641 us -> 85.5 us (0.13)
  waiting for transfers between devices: 596 us -> 0 us
  Pallas kernels: 0 us -> 81.1 us
  matrix products: 24.8 us -> 0 us
  between operations: 13.8 us -> 0.66 us
    reduce_scatter x2 -> x0, waiting for transfers between devices: 419 us -> none  [the longest x1 333 us: body(): lax.psum_scatter(contract_first(selected, projected), 'fsdp', scatter_dim...]
    all_gather x2 -> x0, waiting for transfers between devices: 176 us -> none  [the longest x1 89.3 us: body(): lax.all_gather(activations, 'tp', axis=1, tiled=True)]
    pallas_call x0 -> x1, Pallas kernels: none -> 81.1 us  [body(): pl.pallas_call(kernel, name='galore_step', out_shape=(jax.ShapeDtypeStruc...]
    dot_general x2 -> x0, matrix products: 24.8 us -> none  [the longest x1 19.2 us: contract_first(): lax.dot_general(left_side, right_side, (((0,), (0,)), ((), ())), preferre...]
  transfers between devices with their start and end apart: 4 -> 0, of which waited for: 4 -> 0; matrix products, arithmetic and copies ran while one was open for 0% -> 0% of each run, Pallas kernels for 0% -> 0%
where the time goes in v2:
time: 85.5 us; the launch traced here: 85.4 us
  Pallas kernels  81.1 us (95%)
  local copies, waits for them, and re-layouts  3.62 us (4%)
    pallas_call x1, Pallas kernels, body(): pl.pallas_call(kernel, name='galore_step', out_shape=(jax.ShapeDtypeStruc...  81.1 us
    unnamed x7, local copies, waits for them, and re-layouts  3.62 us

profile of v2, /device:TPU:1, one launch (start us, length us, event | category | flops | bytes accessed | tf_op | source)
XLA Modules:
  0.0 85.4 jit_solution(12079017867947683413)
XLA Ops:
  0.6 81.1 %galore_step.1 = (f32[2048,128]{1,0:T(8,128)}, f32[128,256]{1,0:T(8,128)}, f32[128,256]{1,0:T(8,128)}) custom-call(bf16[512,2048]{1,0:T(8,128)(2,1)} %a_hbm.1, bf16[512,2048]{1,0:T(8,128)(2,1)} %c_hbm.1, bf16[8192,256]{1,0:T(8,128)(2,1)} %p_hbm.1, f32[128,256]{1,0:T(8,128)} %m1_hbm.1, f32[128,256]{1,0:T(8,128)} %m2_hbm.1), custom_call_target="tpu_custom_call" | custom-call | flops 4800000000 | bytes 10485760 | tf_op jit(solution)/shard_map/galore_step/pallas_call | solution.py:479
  81.8 0.0 copy-start.1
  81.8 0.0 copy-start
  81.8 2.3 %copy.11 = f32[2048,128]{1,0:T(8,128)} copy(f32[2048,128]{1,0:T(8,128)} %get-tuple-element.6) | data formatting | bytes 2097152
  84.1 0.0 copy-done.1
  84.1 0.7 copy.12
  84.8 0.0 copy-done
  84.8 0.7 copy.13
Async XLA Ops:
  81.8 2.3 %copy-start.1 = (f32[128,256]{1,0:T(8,128)S(1)}, f32[128,256]{1,0:T(8,128)}, u32[]{:S(2)}) copy-start(f32[128,256]{1,0:T(8,128)} %get-tuple-element.7) | copy-start | bytes 393220
  81.8 3.0 %copy-start = (f32[128,256]{1,0:T(8,128)S(1)}, f32[128,256]{1,0:T(8,128)}, u32[]{:S(2)}) copy-start(f32[128,256]{1,0:T(8,128)} %get-tuple-element.8) | copy-start | bytes 393220

commit v3 on v2

--- a/solution.py
+++ b/solution.py
@@ -11,7 +11,8 @@
 WB = 128 - WA
 SHARED = 352
 DIRECT = 2048 - 4 * SHARED
-NEAR = 256
+NEAR_SHARED = (144, 112)
+NEAR_DIRECT = (256, 208)
 
 
 def device(x, y_hi, z, t):
@@ -62,8 +63,7 @@
         pltpu.make_async_copy(m1_hbm, m1_v, lsem.at[5]),
         pltpu.make_async_copy(m2_hbm, m2_v, lsem.at[6]),
     ]
-    for load in loads:
-        load.start()
+    loads[0].start()
 
     barrier = pltpu.get_barrier_semaphore()
     partners = [other_core, at_x(0), at_x(1), at_z(0), at_z(1)]
@@ -86,17 +86,18 @@
             p_own.at[rows, pl.ds(h * 128, 128)], p_v.at[h, t], pcsend.at[h], pcrecv.at[h], other_core
         )
 
-    def rows_of(kind, side, other):
+    def rows_of(h, kind, side, other):
+        whole_rows, near_rows = (DIRECT, NEAR_DIRECT[h]) if kind == 2 else (SHARED, NEAR_SHARED[h])
+        size = near_rows if side == 0 else whole_rows - near_rows
         if kind == 2:
-            return pl.ds(4 * SHARED + side * NEAR, NEAR if side == 0 else DIRECT - NEAR)
+            return pl.ds(4 * SHARED + side * near_rows, size)
         parity = z % 2 if kind == 0 else x % 2
         if other:
             parity = 1 - parity
-        base = kind * 2 * SHARED + parity * SHARED + side * (SHARED // 2)
-        return pl.ds(pl.multiple_of(base, 16), SHARED // 2)
+        return pl.ds(pl.multiple_of(kind * 2 * SHARED + parity * SHARED + side * near_rows, 16), size)
 
     def p_y(h, kind, side, core):
-        rows = rows_of(kind, side, False)
+        rows = rows_of(h, kind, side, False)
         target = (1 - y_lo) * 2 + core
         src = pl.ds(pl.multiple_of(target * 2048 + rows.start, 16), rows.size)
         return remote(
@@ -105,18 +106,18 @@
         )
 
     def p_y_wait(h, kind, side, core):
-        slot = p_v.at[h, (1 - y_lo) * 2 + core, rows_of(kind, side, False)]
+        slot = p_v.at[h, (1 - y_lo) * 2 + core, rows_of(h, kind, side, False)]
         remote(slot, slot, pysend.at[h, kind, side, core], pyrecv.at[h, kind, side, core], other_core).wait_recv()
 
     def p_relay(h, kind, side, core):
-        slot = p_v.at[h, (1 - y_lo) * 2 + core, rows_of(kind, side, False)]
+        slot = p_v.at[h, (1 - y_lo) * 2 + core, rows_of(h, kind, side, False)]
         return remote(
             slot, slot, prsend.at[h, kind, side, core], prrecv.at[h, kind, side, core],
-            at_z(side) if kind == 0 else at_x(side),
+            at_z((side + core) % 2) if kind == 0 else at_x((side + core) % 2),
         )
 
     def p_relay_wait(h, kind, side, core):
-        slot = p_v.at[h, (1 - y_lo) * 2 + core, rows_of(kind, side, True)]
+        slot = p_v.at[h, (1 - y_lo) * 2 + core, rows_of(h, kind, side, True)]
         remote(slot, slot, prsend.at[h, kind, side, core], prrecv.at[h, kind, side, core], other_core).wait_recv()
 
     each = [(core, kind, side) for core in range(2) for kind in range(2) for side in range(2)]
@@ -370,6 +371,8 @@
 
     loads[0].wait()
     p_first(0)
+    for load in (loads[2], loads[1], *loads[3:]):
+        load.start()
     p_core(0).start()
     p_core(1).start()
     loads[2].wait()
@@ -423,15 +426,15 @@
     z_step(zb, 0, 3)
     x_next(1)
     z_step(zb, 1, 1)
+    z_step(za, 0, 1)
     x_sum(1)
-    z_step(za, 0, 1)
     zb_end(0)
+    z_step(za, 0, 2)
     z_step(zb, 1, 2)
-    z_step(za, 0, 2)
     x_end(1)
-    z_step(zb, 1, 3)
     z_step(za, 0, 3)
     z_step(za, 1, 1)
+    z_step(zb, 1, 3)
     za_end(0)
     z_step(za, 1, 2)
     zb_end(1)

time: 85.5 us -> 84 us (0.982)
  Pallas kernels: 81.1 us -> 79.6 us
    pallas_call x1, Pallas kernels: 81.1 us -> 79.6 us  [body(): pl.pallas_call(kernel, name='galore_step', out_shape=(jax.ShapeDtypeStruc...]
where the time goes in v3:
time: 84 us; the launch traced here: 83.9 us
  Pallas kernels  79.6 us (95%)
  local copies, waits for them, and re-layouts  3.62 us (4%)
    pallas_call x1, Pallas kernels, body(): pl.pallas_call(kernel, name='galore_step', out_shape=(jax.ShapeDtypeStruc...  79.6 us
    unnamed x7, local copies, waits for them, and re-layouts  3.62 us

profile of v3, /device:TPU:1, one launch (start us, length us, event | category | flops | bytes accessed | tf_op | source)
XLA Modules:
  0.0 83.9 jit_solution(16515640275099983629)
XLA Ops:
  0.6 79.6 %galore_step.1 = (f32[2048,128]{1,0:T(8,128)}, f32[128,256]{1,0:T(8,128)}, f32[128,256]{1,0:T(8,128)}) custom-call(bf16[512,2048]{1,0:T(8,128)(2,1)} %a_hbm.1, bf16[512,2048]{1,0:T(8,128)(2,1)} %c_hbm.1, bf16[8192,256]{1,0:T(8,128)(2,1)} %p_hbm.1, f32[128,256]{1,0:T(8,128)} %m1_hbm.1, f32[128,256]{1,0:T(8,128)} %m2_hbm.1), custom_call_target="tpu_custom_call" | custom-call | flops 4800000000 | bytes 10485760 | tf_op jit(solution)/shard_map/galore_step/pallas_call | solution.py:482
  80.3 0.0 copy-start.1
  80.3 0.0 copy-start
  80.3 2.3 %copy.11 = f32[2048,128]{1,0:T(8,128)} copy(f32[2048,128]{1,0:T(8,128)} %get-tuple-element.6) | data formatting | bytes 2097152
  82.6 0.0 copy-done.1
  82.6 0.7 copy.12
  83.2 0.0 copy-done
  83.2 0.7 copy.13
Async XLA Ops:
  80.3 2.3 %copy-start.1 = (f32[128,256]{1,0:T(8,128)S(1)}, f32[128,256]{1,0:T(8,128)}, u32[]{:S(2)}) copy-start(f32[128,256]{1,0:T(8,128)} %get-tuple-element.7) | copy-start | bytes 393220
  80.3 3.0 %copy-start = (f32[128,256]{1,0:T(8,128)S(1)}, f32[128,256]{1,0:T(8,128)}, u32[]{:S(2)}) copy-start(f32[128,256]{1,0:T(8,128)} %get-tuple-element.8) | copy-start | bytes 393220

commit v4 on v3

--- a/solution.py
+++ b/solution.py
@@ -244,8 +244,7 @@
                     + xin[h, yh, 2, k].astype(F32)
                     + xin[h, 1 - yh, 1, k].astype(F32)
                 ).astype(BF)
-        for d in range(2):
-            z_msg(za, h, d, 0).start()
+        z_start(za, h)
 
     def zc(d, n):
         return lax.rem(z + (n if d == 0 else 8 - n), 8)
@@ -257,6 +256,9 @@
         data, first, later, ss, rs = ring
         if m == 0:
             src, dst = data.at[h, zc(d, 4), d], first.at[h, d]
+        elif m in (1, 4):
+            half = d if m == 1 else 1 - d
+            src, dst = data.at[h, zc(d, 3), half], later.at[h, d, 0, half]
         else:
             src, dst = data.at[h, zc(d, 4 - m)], later.at[h, d, m - 1]
         return remote(src, dst, ss.at[h, d, m], rs.at[h, d, m], at_z(d))
@@ -264,11 +266,15 @@
     def z_start(ring, h):
         for d in range(2):
             z_msg(ring, h, d, 0).start()
+        for d in range(2):
+            z_msg(ring, h, d, 4).start()
 
     def z_step(ring, h, m):
         data, first, later, _, _ = ring
         for d in range(2):
             z_msg(ring, h, d, m - 1).wait_recv()
+            if m == 2:
+                z_msg(ring, h, d, 4).wait_recv()
             if m == 1:
                 add(data.at[h, zc(d, 3), d], first.at[h, d])
             else:
@@ -460,7 +466,7 @@
         for d in range(2):
             for m in (1, 2):
                 x_msg(h, d, m).wait_send()
-            for m in range(4):
+            for m in range(5):
                 z_msg(zb, h, d, m).wait_send()
                 z_msg(za, h, d, m).wait_send()
         for yh in range(2):
@@ -521,8 +527,8 @@
             dma((2, 2, 2, 2)), dma((2, 2, 2, 2)),
             dma((3, 2, 2)), dma((3, 2, 2)),
             dma((2, 2, 3)), dma((2, 2, 3)),
-            dma((2, 2, 4)), dma((2, 2, 4)),
-            dma((2, 2, 4)), dma((2, 2, 4)),
+            dma((2, 2, 5)), dma((2, 2, 5)),
+            dma((2, 2, 5)), dma((2, 2, 5)),
             dma((2, 2)), dma((2, 2)),
             dma((2, 4, 2)), dma((2, 8)),
             dma((2, 4)), dma((2, 4)),

time: 84 us -> 83.9 us (level)
  no operation moved by 1% of the time
where the time goes in v4:
time: 83.9 us; the launch traced here: 83.8 us
  Pallas kernels  79.5 us (95%)
  local copies, waits for them, and re-layouts  3.62 us (4%)
    pallas_call x1, Pallas kernels, body(): pl.pallas_call(kernel, name='galore_step', out_shape=(jax.ShapeDtypeStruc...  79.5 us
    unnamed x7, local copies, waits for them, and re-layouts  3.62 us

profile of v4, /device:TPU:1, one launch (start us, length us, event | category | flops | bytes accessed | tf_op | source)
XLA Modules:
  0.0 83.8 jit_solution(2048094095067666581)
XLA Ops:
  0.6 79.5 %galore_step.1 = (f32[2048,128]{1,0:T(8,128)}, f32[128,256]{1,0:T(8,128)}, f32[128,256]{1,0:T(8,128)}) custom-call(bf16[512,2048]{1,0:T(8,128)(2,1)} %a_hbm.1, bf16[512,2048]{1,0:T(8,128)(2,1)} %c_hbm.1, bf16[8192,256]{1,0:T(8,128)(2,1)} %p_hbm.1, f32[128,256]{1,0:T(8,128)} %m1_hbm.1, f32[128,256]{1,0:T(8,128)} %m2_hbm.1), custom_call_target="tpu_custom_call" | custom-call | flops 4800000000 | bytes 10485760 | tf_op jit(solution)/shard_map/galore_step/pallas_call | solution.py:488
  80.1 0.0 copy-start.1
  80.2 0.0 copy-start
  80.2 2.3 %copy.11 = f32[2048,128]{1,0:T(8,128)} copy(f32[2048,128]{1,0:T(8,128)} %get-tuple-element.6) | data formatting | bytes 2097152
  82.5 0.0 copy-done.1
  82.5 0.7 copy.12
  83.1 0.0 copy-done
  83.1 0.7 copy.13
Async XLA Ops:
  80.1 2.3 %copy-start.1 = (f32[128,256]{1,0:T(8,128)S(1)}, f32[128,256]{1,0:T(8,128)}, u32[]{:S(2)}) copy-start(f32[128,256]{1,0:T(8,128)} %get-tuple-element.7) | copy-start | bytes 393220
  80.2 3.0 %copy-start = (f32[128,256]{1,0:T(8,128)S(1)}, f32[128,256]{1,0:T(8,128)}, u32[]{:S(2)}) copy-start(f32[128,256]{1,0:T(8,128)} %get-tuple-element.8) | copy-start | bytes 393220
